TPU v7x, 32 devices: a whole 2x2x4 slice. The times are simulated.
32 devices in a mesh: groups: 2 (over x), space: 8 (over z, y), beam: 2 (over core).
Axes of the slice: x: 2, y: 2, z: 4, core: 2. Of those that a mesh axis runs over, the one named last changes fastest.
Arguments:
- s_matrix: bfloat16 [4096, 256, 480], P(('groups', 'beam'), 'space'), parts along dimension 0, may hold values from -6 to 6
- beam_index: int32 [2048, 2], P('beam'), may hold values from -24 to 23, as said below
- beam_amp: float32 [2048], P('beam'), may hold values from 0.5 to 2
- beam_phase: float32 [2048], P('beam'), may hold values from -3.140625 to 3.140625
- positions: int32 [2, 384, 2], replicated, may hold values from 0 to 239
Outputs:
- intensities: float32 [4, 384, 256, 240], P('groups', ('space', 'beam')), parts along dimension 0
There are 2 independent parts, one for each index of `groups`. A program takes and returns all parts, laid end to end along the dimension named above; an argument that names none is the same for every part. Nothing has to cross between parts.
Inputs may be any that keep to these rules, and one draw needn't show every extreme that they name: `beam_index`: no two beams have the same wave-vector.
All inputs are finite; a program needn't handle non-finite values.
Results may differ from a plain program's by a relative error of at most 0.0072.
Values may be sent and summed in bfloat16 or wider, within the bound.
A program may use at most 192 MiB of HBM per device.

v0:
```python
import math

import jax
import jax.numpy as jnp
from jax import lax
from jax.sharding import PartitionSpec as P

NB = 2048
RY = 256
RX = 240


def dft_tables():
    xs = jnp.arange(RX, dtype=jnp.int32)
    prod_x = jnp.mod(xs[:, None] * xs[None, :], RX).astype(jnp.float32)
    angle_x = 2.0 * math.pi / RX * prod_x
    cos_x = jnp.cos(angle_x) / math.sqrt(RX)
    sin_x = jnp.sin(angle_x) / math.sqrt(RX)
    table_x = jnp.concatenate(
        [jnp.concatenate([cos_x, -sin_x], 1), jnp.concatenate([sin_x, cos_x], 1)], 0
    ).astype(jnp.bfloat16)
    ys = jnp.arange(RY, dtype=jnp.int32)
    prod_y = jnp.mod(ys[:, None] * ys[None, :], RY).astype(jnp.float32)
    angle_y = 2.0 * math.pi / RY * prod_y
    table_y = jnp.concatenate([jnp.cos(angle_y), jnp.sin(angle_y)], 0) / math.sqrt(RY)
    return (table_x, table_y.astype(jnp.bfloat16))


def coefficients(spots, beam_index, beam_amp, beam_phase):
    rows_part = jnp.mod(spots[:, 0:1] * beam_index[None, :, 0], RY).astype(jnp.float32)
    cols_part = jnp.mod(spots[:, 1:2] * beam_index[None, :, 1], RX).astype(jnp.float32)
    theta = beam_phase[None, :] - 2.0 * math.pi * (rows_part / RY + cols_part / RX)
    scale = beam_amp[None, :] / math.sqrt(NB)
    return (
        (scale * jnp.cos(theta)).astype(jnp.bfloat16),
        (scale * jnp.sin(theta)).astype(jnp.bfloat16),
    )


def body(s_matrix, beam_index, beam_amp, beam_phase, positions):
    local_beams = s_matrix.shape[0]
    local_rows = s_matrix.shape[1]
    n_space = lax.axis_size("space")
    n_beam = lax.axis_size("beam")
    n_batch = positions.shape[0]
    per_device = positions.shape[1] // (n_space * n_beam)
    flat_s = s_matrix.reshape(local_beams, local_rows * 2 * RX)
    table_x, table_y = dft_tables()

    def transform(wave, count):
        half = jnp.dot(wave.reshape(-1, 2 * RX), table_x, preferred_element_type=jnp.float32)
        half = half.astype(jnp.bfloat16).reshape(-1, RY, 2 * RX)
        spectrum = jnp.einsum("vy,pyc->pvc", table_y, half, preferred_element_type=jnp.float32)
        spec_re = spectrum[:, :RY, :RX] + spectrum[:, RY:, RX:]
        spec_im = spectrum[:, :RY, RX:] - spectrum[:, RY:, :RX]
        return (spec_re * spec_re + spec_im * spec_im).reshape(count, per_device, RY, RX)

    def one_group(chosen):
        count = chosen.shape[0]
        blocks = chosen.reshape(count, n_space, n_beam, per_device, 2)
        spots = jnp.transpose(blocks, (2, 1, 0, 3, 4)).reshape(-1, 2)
        coef_re, coef_im = coefficients(spots, beam_index, beam_amp, beam_phase)
        total_rows = spots.shape[0]
        product = jnp.dot(
            jnp.concatenate([coef_re, coef_im], 0), flat_s, preferred_element_type=jnp.float32
        )
        product = product.reshape(
            2, total_rows // n_beam * lax.axis_size("beam"), local_rows, 2 * RX
        )
        wave_re = product[0, ..., :RX] - product[1, ..., RX:]
        wave_im = product[0, ..., RX:] + product[1, ..., :RX]
        rounded = lax.optimization_barrier(
            jnp.concatenate([wave_re, wave_im], -1).astype(jnp.bfloat16)
        )
        summed = lax.psum_scatter(
            rounded.astype(jnp.float32).astype(jnp.bfloat16),
            "beam",
            scatter_dimension=0,
            tiled=True,
        )
        wave = lax.all_to_all(summed, "space", split_axis=0, concat_axis=1, tiled=True)
        return transform(wave, count)

    outputs = [one_group(positions[batch : batch + 1]) for batch in range(n_batch)]
    return jnp.concatenate(outputs, 0)


def solution(mesh):
    in_specs = (P(("groups", "beam"), "space", None), P("beam", None), P("beam"), P("beam"), P())
    out_specs = P("groups", ("space", "beam"), None, None)
    return jax.shard_map(body, mesh=mesh, in_specs=in_specs, out_specs=out_specs, check_vma=False)
```

profile of v0, /device:TPU:0, one launch (start us, length us, event | category | flops | bytes accessed | tf_op | source)
XLA Modules:
  0.0 513.2 jit_solution(4622857411658525311)
XLA Ops:
  9.2 16.0 %multiply_convert_fusion.3 = (bf16[384,1024]{1,0:T(8,128)(2,1)S(1)}, bf16[384,1024]{1,0:T(8,128)(2,1)S(1)}, bf16[384,1024]{1,0:T(8,128)(2,1)S(1)}, bf16[384,1024]{1,0:T(8,128)(2,1)S(1)}) fusion(s32[1024]{0:T(1024)S(1)} %bitcast.92, s32[384]{0:T(512)S(1)} %get-tuple-element.6, s32[1024]{0:T(1024)S(1)} %bitcast.91, s32[384]{0:T(512)S(1)} %get-tuple-element.5, ...), kind=kLoop, calls=%fused_computation.75 | loop fusion | flops 23592960 | bytes 3168256 | tf_op jit(solution)/shard_map/convert_element_type | solution.py:35
  25.2 1.5 pad_maximum_fusion.3
  26.7 34.1 %fusion = f32[2,384,32,480]{1,3,2,0:T(8,128)} fusion(bf16[2,384,1024,1]{2,1,3,0:T(8,128)(2,1)S(1)} %bitcast.88, bf16[1024,32,480]{0,2,1:T(8,128)(2,1)} %param.5), kind=kOutput, calls=%fused_computation | convolution fusion | flops 24159191040 | bytes 80216064 | tf_op jit(solution)/shard_map/dot_general | solution.py:64
  60.7 15.8 %fusion.10 = (bf16[384,32,240]{0,2,1:T(8,128)(2,1)S(1)}, bf16[384,32,240]{0,2,1:T(8,128)(2,1)S(1)}) fusion(f32[2,384,32,480]{1,3,2,0:T(8,128)} %fusion), kind=kLoop, calls=%fused_computation.21 | loop fusion | flops 11796480 | bytes 58982400 | tf_op jit(solution)/shard_map/sub | solution.py:70
  76.5 5.5 %pad_maximum_fusion.1 = bf16[384,32,480]{0,2,1:T(8,128)(2,1)} fusion(bf16[384,32,240]{0,2,1:T(8,128)(2,1)S(1)} %get-tuple-element.12, bf16[384,32,240]{0,2,1:T(8,128)(2,1)S(1)} %get-tuple-element.11), kind=kLoop, calls=%fused_computation.13 | loop fusion | flops 23592960 | bytes 23592960 | tf_op jit(solution)/shard_map/concatenate | solution.py:73
  82.0 16.8 %copy.21 = bf16[384,32,480]{2,1,0:T(8,128)(2,1)} copy(bf16[384,32,480]{0,2,1:T(8,128)(2,1)} %pad_maximum_fusion.1) | data formatting | bytes 23592960 | tf_op jit(solution)/shard_map/optimization_barrier | solution.py:72
  100.2 36.5 %fusion.2 = f32[2,384,32,480]{1,3,2,0:T(8,128)} fusion(bf16[2,384,1024,1]{2,1,3,0:T(8,128)(2,1)S(1)} %bitcast.87, bf16[1024,32,480]{0,2,1:T(8,128)(2,1)} %param.5), kind=kOutput, calls=%fused_computation.2 | convolution fusion | flops 24159191040 | bytes 80216064 | tf_op jit(solution)/shard_map/dot_general | solution.py:64
  136.7 15.8 %fusion.8 = (bf16[384,32,240]{0,2,1:T(8,128)(2,1)S(1)}, bf16[384,32,240]{0,2,1:T(8,128)(2,1)S(1)}) fusion(f32[2,384,32,480]{1,3,2,0:T(8,128)} %fusion.2), kind=kLoop, calls=%fused_computation.19 | loop fusion | flops 11796480 | bytes 58982400 | tf_op jit(solution)/shard_map/sub | solution.py:70
  152.5 5.5 %pad_maximum_fusion = bf16[384,32,480]{0,2,1:T(8,128)(2,1)} fusion(bf16[384,32,240]{0,2,1:T(8,128)(2,1)S(1)} %get-tuple-element.10, bf16[384,32,240]{0,2,1:T(8,128)(2,1)S(1)} %get-tuple-element.9), kind=kLoop, calls=%fused_computation.12 | loop fusion | flops 23592960 | bytes 23592960 | tf_op jit(solution)/shard_map/concatenate | solution.py:73
  158.0 16.6 %copy.17 = bf16[384,32,480]{2,1,0:T(8,128)(2,1)} copy(bf16[384,32,480]{0,2,1:T(8,128)(2,1)} %pad_maximum_fusion) | data formatting | bytes 23592960 | tf_op jit(solution)/shard_map/optimization_barrier | solution.py:72
  174.7 6.8 %all-to-all-start.1 = ((bf16[192,32,480]{2,1,0:T(8,128)(2,1)}), bf16[192,32,480]{2,1,0:T(8,128)(2,1)}, u32[]{:S(2)}, u32[]{:S(2)}) async-start(bf16[192,32,480]{2,1,0:T(8,128)(2,1)} %reduce-scatter.5.cloned.1.call-done), calls=%async_computation.3 | async-start | bytes 12582912 | tf_op jit(solution)/shard_map/all_to_all | solution.py:81
  181.5 17.0 %reduce-scatter.3.cloned.1.call-done = bf16[192,32,480]{2,1,0:T(8,128)(2,1)} async-done(((bf16[384,32,480]{2,1,0:T(8,128)(2,1)}), bf16[192,32,480]{2,1,0:T(8,128)(2,1)}) %reduce-scatter.3.cloned.1.call-update) | async-done | bytes 5898256 | tf_op jit(solution)/shard_map/reduce_scatter | solution.py:75
  198.5 121.2 %all-to-all-done.1 = bf16[192,32,480]{2,1,0:T(8,128)(2,1)} async-done(((bf16[192,32,480]{2,1,0:T(8,128)(2,1)}), bf16[192,32,480]{2,1,0:T(8,128)(2,1)}, u32[]{:S(2)}, u32[]{:S(2)}) %all-to-all-start.1) | async-done | bytes 5898272 | tf_op jit(solution)/shard_map/all_to_all | solution.py:81
  319.7 5.0 all-to-all-start
  327.8 3.4 copy.22
  331.2 4.0 convolution_convert_fusion
  335.3 9.6 %convolution_bitcast_fusion = f32[24,512,480]{1,2,0:T(8,128)} fusion(bf16[60,24,8,256]{3,2,1,0:T(8,128)(2,1)S(1)} %bitcast.82, f32[256,256]{1,0:T(8,128)S(1)} %get-tuple-element.27, f32[256,256]{1,0:T(8,128)S(1)} %get-tuple-element.28), kind=kOutput, calls=%fused_computation.17 | convolution fusion | flops 3020292096 | bytes 30015488 | tf_op jit(solution)/shard_map/vy,pyc->pvc/dot_general | solution.py:53
  344.9 11.4 %fusion.18 = f32[1,24,256,240]{2,3,1,0:T(8,128)} fusion(f32[24,512,480]{1,2,0:T(8,128)} %convolution_bitcast_fusion), kind=kLoop, calls=%fused_computation.30 | loop fusion | flops 7372800 | bytes 29491200 | tf_op jit(solution)/shard_map/reshape | solution.py:56
  356.3 105.5 %all-to-all-done = bf16[192,32,480]{2,1,0:T(8,128)(2,1)} async-done(((bf16[192,32,480]{2,1,0:T(8,128)(2,1)}), bf16[192,32,480]{2,1,0:T(8,128)(2,1)}, u32[]{:S(2)}, u32[]{:S(2)}) %all-to-all-start) | async-done | bytes 5898272 | tf_op jit(solution)/shard_map/all_to_all | solution.py:81
  461.8 6.6 %copy.18 = bf16[24,8,32,480]{3,2,1,0:T(8,128)(2,1)} copy(bf16[24,8,32,480]{3,2,0,1:T(8,128)(2,1)} %bitcast.13) | data formatting | bytes 11796480 | tf_op jit(solution)/shard_map/all_to_all | solution.py:81
  468.4 8.7 %convolution_convert_fusion.1 = bf16[6144,480]{0,1:T(8,128)(2,1)S(1)} fusion(bf16[6144,480]{1,0:T(8,128)(2,1)} %bitcast.85, bf16[240,240]{1,0:T(8,128)(2,1)S(1)} %get-tuple-element.26, bf16[240,240]{1,0:T(8,128)(2,1)S(1)} %fusion.59, bf16[240,240]{1,0:T(8,128)(2,1)S(1)} %get-tuple-element.25), kind=kOutput, calls=%fused_computation.16 | convolution fusion | flops 2835947520 | bytes 12142080 | tf_op jit(solution)/shard_map/dot_general | solution.py:51
  477.1 9.9 %convolution_bitcast_fusion.1 = f32[24,512,480]{1,2,0:T(8,128)} fusion(bf16[60,24,8,256]{3,2,1,0:T(8,128)(2,1)S(1)} %bitcast.81, f32[256,256]{1,0:T(8,128)S(1)} %get-tuple-element.27, f32[256,256]{1,0:T(8,128)S(1)} %get-tuple-element.28), kind=kOutput, calls=%fused_computation.18 | convolution fusion | flops 3020292096 | bytes 30015488 | tf_op jit(solution)/shard_map/vy,pyc->pvc/dot_general | solution.py:53
  487.0 11.4 %fusion.22 = f32[1,24,256,240]{2,3,1,0:T(8,128)} fusion(f32[24,512,480]{1,2,0:T(8,128)} %convolution_bitcast_fusion.1), kind=kLoop, calls=%fused_computation.36 | loop fusion | flops 7372800 | bytes 29491200 | tf_op jit(solution)/shard_map/reshape | solution.py:56
  498.4 8.0 %pad_maximum_fusion.2 = f32[2,24,256,240]{2,3,1,0:T(8,128)} fusion(f32[1,24,256,240]{2,3,1,0:T(8,128)S(1)} %bitcast.84, f32[1,24,256,240]{2,3,1,0:T(8,128)} %fusion.22), kind=kLoop, calls=%fused_computation.14 | loop fusion | flops 2949120 | bytes 23592960 | tf_op jit(solution)/shard_map/concatenate | solution.py:85
  (26 shorter events, 7.1 us)
Async XLA Ops:
  6.5 168.2 %reduce-scatter.5.cloned.1.call-start = ((), (), s32[]{:S(2)}) async-start(), calls=%async_computation.5 | async-start | bytes 18874368 | tf_op jit(solution)/shard_map/reduce_scatter | solution.py:75
  98.8 1.4 copy-start
  98.8 99.7 %reduce-scatter.3.cloned.1.call-start = ((), (), s32[]{:S(2)}) async-start(), calls=%async_computation.4 | async-start | bytes 18874368 | tf_op jit(solution)/shard_map/reduce_scatter | solution.py:75
  174.7 145.0 %all-to-all-start.1 = ((bf16[192,32,480]{2,1,0:T(8,128)(2,1)}), bf16[192,32,480]{2,1,0:T(8,128)(2,1)}, u32[]{:S(2)}, u32[]{:S(2)}) async-start(bf16[192,32,480]{2,1,0:T(8,128)(2,1)} %reduce-scatter.5.cloned.1.call-done), calls=%async_computation.3 | async-start | bytes 12582912 | tf_op jit(solution)/shard_map/all_to_all | solution.py:81
  319.7 142.0 %all-to-all-start = ((bf16[192,32,480]{2,1,0:T(8,128)(2,1)}), bf16[192,32,480]{2,1,0:T(8,128)(2,1)}, u32[]{:S(2)}, u32[]{:S(2)}) async-start(bf16[192,32,480]{2,1,0:T(8,128)(2,1)} %reduce-scatter.3.cloned.1.call-done), calls=%async_computation.1 | async-start | bytes 12582912 | tf_op jit(solution)/shard_map/all_to_all | solution.py:81
  468.4 29.9 %slice-start = ((s8[5898240]{0:T(1024)(128)(4,1)}), s8[4194304]{0:T(1024)(128)(4,1)S(1)}, s32[]{:S(2)}) async-start(s8[5898240]{0:T(1024)(128)(4,1)} %bitcast.83), calls=%async_computation.6 | async-start | bytes 8388608
  477.1 21.3 %slice-start.1 = ((s8[5898240]{0:T(1024)(128)(4,1)}), s8[1703936]{0:T(1024)(128)(4,1)S(1)}, s32[]{:S(2)}) async-start(s8[5898240]{0:T(1024)(128)(4,1)} %bitcast.83), calls=%async_computation.7 | async-start | bytes 3407872
Sparse Core Ops, SparseCore 0:
  99.0 24.1 reduce-scatter.4
  174.8 23.6 reduce-scatter.2
where the time goes:
time: 515 us; the launch traced here: 513 us
  waiting for transfers between devices  244 us (47%)
  matrix products  103 us (20%)
  other arithmetic  94.6 us (18%)
  local copies, waits for them, and re-layouts  46.4 us (9%)
  between operations  13.6 us (3%)
  starting transfers between devices  12 us (2%)
    all_to_all x2, waiting for transfers between devices, one_group(): lax.all_to_all(summed, 'space', split_axis=0, concat_axis=1, tiled=True)  227 us
    dot_general x2, matrix products, one_group(): jnp.dot(jnp.concatenate([coef_re, coef_im], 0), flat_s, preferred_element...  70.6 us
    optimization_barrier x2, local copies, waits for them, and re-layouts, one_group(): lax.optimization_barrier(jnp.concatenate([wave_re, wave_im], -1).astype(j...  33.4 us
    sub x2, other arithmetic, one_group(): wave_re = product[0, ..., :RX] - product[1, ..., RX:]  31.6 us
    reshape x2, other arithmetic, transform(): (spec_re * spec_re + spec_im * spec_im).reshape(count, per_device, RY, RX)  22.7 us
    dot_general x2, matrix products, transform(): jnp.einsum('vy,pyc->pvc', table_y, half, preferred_element_type=jnp.float32)  19.5 us
    reduce_scatter x2, waiting for transfers between devices, one_group(): lax.psum_scatter(rounded.astype(jnp.float32).astype(jnp.bfloat16), 'beam'...  17 us
    convert_element_type x1, other arithmetic, coefficients(): (scale * jnp.cos(theta)).astype(jnp.bfloat16)  16 us
  transfers between devices with their start and end apart: 4, of which 3 were waited for; matrix products, arithmetic and copies ran while one was open for 21% of the time, Pallas kernels for 0%

commit v1 on v0

v1 whole, which is shorter than its diff:
```python
import functools
import math

import jax
import jax.numpy as jnp
from jax import lax
from jax.experimental import pallas as pl
from jax.experimental.pallas import tpu as pltpu
from jax.sharding import PartitionSpec as P

VMEM = 56 * 1024 * 1024


def dft_tables(rows, cols, n_space, pack):
    xs = jnp.arange(cols, dtype=jnp.int32)
    prod_x = jnp.mod(xs[:, None] * xs[None, :], cols).astype(jnp.float32)
    angle_x = 2.0 * math.pi / cols * prod_x
    cos_x = jnp.cos(angle_x) / math.sqrt(cols)
    sin_x = jnp.sin(angle_x) / math.sqrt(cols)
    table_x = jnp.concatenate(
        [jnp.concatenate([cos_x, -sin_x], 1), jnp.concatenate([sin_x, cos_x], 1)], 0
    ).astype(jnp.bfloat16)
    ys = jnp.arange(rows, dtype=jnp.int32)
    order = ys.reshape(n_space, pack, -1).transpose(1, 0, 2).reshape(-1)
    prod_y = jnp.mod(order[:, None] * ys[None, :], rows).astype(jnp.float32)
    angle_y = 2.0 * math.pi / rows * prod_y
    table_y = jnp.concatenate([jnp.cos(angle_y), jnp.sin(angle_y)], 1) / math.sqrt(rows)
    return table_x, table_y.astype(jnp.bfloat16)


def coefficients(spots, beam_index, beam_amp, beam_phase, rows, cols, n_beams):
    rows_part = jnp.mod(spots[:, 0:1] * beam_index[None, :, 0], rows).astype(jnp.float32)
    cols_part = jnp.mod(spots[:, 1:2] * beam_index[None, :, 1], cols).astype(jnp.float32)
    theta = beam_phase[None, :] - 2.0 * math.pi * (rows_part / rows + cols_part / cols)
    scale = beam_amp[None, :] / math.sqrt(n_beams)
    return jnp.concatenate(
        [(scale * jnp.cos(theta)).astype(jnp.bfloat16), (scale * jnp.sin(theta)).astype(jnp.bfloat16)], 0
    )


def gemm_kernel(c_ref, s_ref, o_ref):
    n_rows, width, _ = s_ref.shape
    cols = width // 2
    n_beam, _, per, _ = o_ref.shape
    probes = n_beam * per
    dims = (((1,), (1,)), ((), ()))
    for y in range(n_rows):
        on_re = lax.dot_general(c_ref[...], s_ref[y, :cols, :], dims, preferred_element_type=jnp.float32)
        on_im = lax.dot_general(c_ref[...], s_ref[y, cols:, :], dims, preferred_element_type=jnp.float32)
        wave_re = (on_re[:probes] - on_im[probes:]).astype(jnp.bfloat16)
        wave_im = (on_im[:probes] + on_re[probes:]).astype(jnp.bfloat16)
        for h in range(n_beam):
            o_ref[h, y, :, :cols] = wave_re[h * per:(h + 1) * per]
            o_ref[h, y, :, cols:] = wave_im[h * per:(h + 1) * per]


def waves(coef, s_rows, n_beam):
    local_rows, width, beams = s_rows.shape
    probes = coef.shape[0] // 2
    block = 4
    return pl.pallas_call(
        gemm_kernel,
        grid=(local_rows // block,),
        in_specs=[
            pl.BlockSpec((2 * probes, beams), lambda i: (0, 0)),
            pl.BlockSpec((block, width, beams), lambda i: (i, 0, 0)),
        ],
        out_specs=pl.BlockSpec((n_beam, block, probes // n_beam, width), lambda i: (0, i, 0, 0)),
        out_shape=jax.ShapeDtypeStruct((n_beam, local_rows, probes // n_beam, width), jnp.bfloat16),
        compiler_params=pltpu.CompilerParams(vmem_limit_bytes=VMEM),
        cost_estimate=pl.CostEstimate(
            flops=4 * probes * beams * local_rows * width,
            bytes_accessed=2 * local_rows * width * beams,
            transcendentals=0,
        ),
        name="waves",
    )(coef, s_rows)


def half_kernel(pack, w_ref, t_ref, o_ref):
    local_rows, per, width = w_ref.shape
    half = jnp.dot(w_ref[...].reshape(local_rows * per, width), t_ref[...], preferred_element_type=jnp.float32)
    half = jnp.swapaxes(half.reshape(local_rows, per, width), 0, 1)
    part = local_rows // pack
    for q in range(pack):
        o_ref[:, :, q * width:(q + 1) * width] = half[:, q * part:(q + 1) * part, :].astype(jnp.bfloat16)


def halves(wave, table_x, pack):
    local_rows, per, width = wave.shape
    return pl.pallas_call(
        functools.partial(half_kernel, pack),
        out_shape=jax.ShapeDtypeStruct((per, local_rows // pack, pack * width), jnp.bfloat16),
        compiler_params=pltpu.CompilerParams(vmem_limit_bytes=VMEM),
        cost_estimate=pl.CostEstimate(
            flops=2 * per * local_rows * width * width,
            bytes_accessed=4 * per * local_rows * width,
            transcendentals=0,
        ),
        name="halves",
    )(wave, table_x)


def spectrum_kernel(pack, h_ref, t_ref, *rest):
    o_ref = rest[-1]
    n_space, _, part, packed = h_ref.shape
    width = packed // pack
    cols = width // 2
    rows = n_space * part * pack
    block = h_ref[:, 0].reshape(n_space * part, packed)
    half = jnp.concatenate([block[:, q * width:(q + 1) * width] for q in range(pack)], 0)
    both = lax.dot_general(half, t_ref[...], (((0,), (0,)), ((), ())), preferred_element_type=jnp.float32)
    spec_re = both[:cols, :rows] + both[cols:, rows:]
    spec_im = both[cols:, :rows] - both[:cols, rows:]
    o_ref[0] = spec_re * spec_re + spec_im * spec_im


def spectra(half, table_y, out, first, total, pack):
    n_space, count, part, packed = half.shape
    rows = n_space * part * pack
    cols = packed // pack // 2
    operands = [half, table_y]
    in_specs = [
        pl.BlockSpec((n_space, 1, part, packed), lambda i: (0, i, 0, 0)),
        pl.BlockSpec((rows, 2 * rows), lambda i: (0, 0)),
    ]
    if out is not None:
        operands.append(out)
        in_specs.append(pl.BlockSpec(memory_space=pl.ANY))
    return pl.pallas_call(
        functools.partial(spectrum_kernel, pack),
        grid=(count,),
        in_specs=in_specs,
        out_specs=pl.BlockSpec((1, cols, rows), lambda i: (first + i, 0, 0)),
        out_shape=jax.ShapeDtypeStruct((total, cols, rows), jnp.float32),
        input_output_aliases={} if out is None else {2: 0},
        compiler_params=pltpu.CompilerParams(vmem_limit_bytes=VMEM),
        cost_estimate=pl.CostEstimate(
            flops=8 * count * cols * rows * rows,
            bytes_accessed=8 * count * cols * rows,
            transcendentals=0,
        ),
        name="spectra",
    )(*operands)


def body(s_matrix, beam_index, beam_amp, beam_phase, positions):
    n_space = lax.axis_size("space")
    n_beam = lax.axis_size("beam")
    local_beams, local_rows, width = s_matrix.shape
    cols = width // 2
    rows = local_rows * n_space
    n_batch = positions.shape[0]
    per_device = positions.shape[1] // (n_space * n_beam)
    pack = 4 if local_rows % 32 == 0 else 1
    n_chunk = 3
    count = per_device // n_chunk
    s_rows = jnp.transpose(s_matrix, (1, 2, 0))
    table_x, table_y = dft_tables(rows, cols, n_space, pack)
    blocks = positions.reshape(n_batch, n_space, n_beam, n_chunk, count, 2)
    blocks = jnp.transpose(blocks, (0, 3, 2, 1, 4, 5)).reshape(n_batch * n_chunk, -1, 2)

    out = None
    for chunk in range(n_batch * n_chunk):
        coef = coefficients(
            blocks[chunk], beam_index, beam_amp, beam_phase, rows, cols, local_beams * n_beam
        )
        partial = waves(coef, s_rows, n_beam)
        wave = lax.psum_scatter(partial, "beam", scatter_dimension=0, tiled=True)[0]
        half = halves(wave, table_x, pack)
        half = lax.all_to_all(half, "space", split_axis=0, concat_axis=0, tiled=True)
        half = half.reshape(n_space, count, local_rows // pack, pack * width)
        out = spectra(half, table_y, out, chunk * count, n_batch * per_device, pack)
    out = out.reshape(n_batch, per_device, cols, rows)
    return jnp.swapaxes(out, 2, 3)


def solution(mesh):
    in_specs = (P(("groups", "beam"), "space", None), P("beam", None), P("beam"), P("beam"), P())
    out_specs = P("groups", ("space", "beam"), None, None)
    return jax.shard_map(body, mesh=mesh, in_specs=in_specs, out_specs=out_specs, check_vma=False)
```

time: 515 us -> 425 us (0.83)
  Pallas kernels: 0 us -> 180 us
  matrix products: 103 us -> 0 us
  waiting for transfers between devices: 244 us -> 171 us
  other arithmetic: 94.6 us -> 26.4 us
  local copies, waits for them, and re-layouts: 46.4 us -> 1.85 us
  starting transfers between devices: 12 us -> 28.5 us
    pallas_call x0 -> x18, Pallas kernels: none -> 180 us  [the longest x6 106 us: waves(): pl.pallas_call(gemm_kernel, grid=(local_rows // block,), in_specs=[pl.Blo...]
    dot_general x6 -> x0, matrix products: 103 us -> none  [the longest x2 70.6 us: one_group(): jnp.dot(jnp.concatenate([coef_re, coef_im], 0), flat_s, preferred_element...]
    all_to_all x2 -> x6, waiting for transfers between devices: 227 us -> 171 us  [body(): lax.all_to_all(half, 'space', split_axis=0, concat_axis=0, tiled=True)]
    optimization_barrier x2 -> x0, local copies, waits for them, and re-layouts: 33.4 us -> none  [one_group(): lax.optimization_barrier(jnp.concatenate([wave_re, wave_im], -1).astype(j...]
    sub x2 -> x0, other arithmetic: 31.6 us -> none  [one_group(): wave_re = product[0, ..., :RX] - product[1, ..., RX:]]
    reshape x2 -> x1, other arithmetic: 22.7 us -> 0.01 us  [dft_tables(): order = ys.reshape(n_space, pack, -1).transpose(1, 0, 2).reshape(-1)]
    reduce_scatter x2 -> x6, waiting for transfers between devices: 17 us -> 0.1 us  [body(): wave = lax.psum_scatter(partial, 'beam', scatter_dimension=0, tiled=True)[0]]
    all_to_all x2 -> x6, starting transfers between devices: 11.8 us -> 27.9 us  [body(): lax.all_to_all(half, 'space', split_axis=0, concat_axis=0, tiled=True)]
  transfers between devices with their start and end apart: 4 -> 12, of which waited for: 3 -> 6; matrix products, arithmetic and copies ran while one was open for 21% -> 2% of each run, Pallas kernels for 0% -> 37%
where the time goes in v1:
time: 425 us; the launch traced here: 422 us
  Pallas kernels  180 us (42%)
  waiting for transfers between devices  171 us (40%)
  starting transfers between devices  28.5 us (7%)
  other arithmetic  26.4 us (6%)
  between operations  13.6 us (3%)
    all_to_all x6, waiting for transfers between devices, body(): lax.all_to_all(half, 'space', split_axis=0, concat_axis=0, tiled=True)  171 us
    pallas_call x6, Pallas kernels, waves(): pl.pallas_call(gemm_kernel, grid=(local_rows // block,), in_specs=[pl.Blo...  106 us
    pallas_call x6, Pallas kernels, spectra(): pl.pallas_call(functools.partial(spectrum_kernel, pack), grid=(count,), i...  44.1 us
    pallas_call x6, Pallas kernels, halves(): pl.pallas_call(functools.partial(half_kernel, pack), out_shape=jax.ShapeD...  29.8 us
    all_to_all x6, starting transfers between devices, body(): lax.all_to_all(half, 'space', split_axis=0, concat_axis=0, tiled=True)  27.9 us
    convert_element_type x1, other arithmetic, coefficients(): (scale * jnp.cos(theta)).astype(jnp.bfloat16)  15.7 us
  transfers between devices with their start and end apart: 12, of which 6 were waited for; matrix products, arithmetic and copies ran while one was open for 2% of the time, Pallas kernels for 37%

profile of v1, /device:TPU:0, one launch (start us, length us, event | category | flops | bytes accessed | tf_op | source)
XLA Modules:
  0.0 421.9 jit_solution(2778500009177369295)
XLA Ops:
  9.0 15.7 %multiply_convert_fusion.1 = (bf16[128,1024]{1,0:T(8,128)(2,1)S(1)}, bf16[128,1024]{1,0:T(8,128)(2,1)S(1)}, bf16[128,1024]{1,0:T(8,128)(2,1)S(1)}, bf16[128,1024...) fusion(s32[1024]{0:T(1024)S(1)} %bitcast.78, ...), kind=kLoop, calls=%fused_computation.93 | loop fusion | flops 23592960 | bytes 3168256 | tf_op jit(solution)/shard_map/convert_element_type | solution.py:37
  25.6 17.3 %waves.11 = bf16[2,32,64,480]{3,2,1,0:T(8,128)(2,1)} custom-call(bf16[256,1024]{1,0:T(8,128)(2,1)} %pad_maximum_fusion.5.c_ref, bf16[32,480,1024]{2,1,0:T(8,128)(2,1)} %bitcast.61), custom_call_target="tpu_custom_call" | custom-call | flops 8053063680 | bytes 31457280 | tf_op jit(solution)/shard_map/waves/pallas_call | solution.py:61
  43.8 18.1 %waves.10 = bf16[2,32,64,480]{3,2,1,0:T(8,128)(2,1)} custom-call(bf16[256,1024]{1,0:T(8,128)(2,1)} %pad_maximum_fusion.4.c_ref, bf16[32,480,1024]{2,1,0:T(8,128)(2,1)} %bitcast.62), custom_call_target="tpu_custom_call" | custom-call | flops 8053063680 | bytes 31457280 | tf_op jit(solution)/shard_map/waves/pallas_call | solution.py:61
  62.8 18.2 %waves.9 = bf16[2,32,64,480]{3,2,1,0:T(8,128)(2,1)} custom-call(bf16[256,1024]{1,0:T(8,128)(2,1)} %pad_maximum_fusion.3.c_ref, bf16[32,480,1024]{2,1,0:T(8,128)(2,1)} %bitcast.63), custom_call_target="tpu_custom_call" | custom-call | flops 8053063680 | bytes 31457280 | tf_op jit(solution)/shard_map/waves/pallas_call | solution.py:61
  82.1 18.1 %waves.8 = bf16[2,32,64,480]{3,2,1,0:T(8,128)(2,1)} custom-call(bf16[256,1024]{1,0:T(8,128)(2,1)} %pad_maximum_fusion.2.c_ref, bf16[32,480,1024]{2,1,0:T(8,128)(2,1)} %bitcast.64), custom_call_target="tpu_custom_call" | custom-call | flops 8053063680 | bytes 31457280 | tf_op jit(solution)/shard_map/waves/pallas_call | solution.py:61
  103.3 5.0 %halves.11 = bf16[64,8,1920]{2,1,0:T(8,128)(2,1)} custom-call(bf16[32,64,480]{2,1,0:T(8,128)(2,1)} %bitcast.74, bf16[480,480]{1,0:T(8,128)(2,1)} %maximum_maximum_fusion.t_ref), custom_call_target="tpu_custom_call" | custom-call | flops 943718400 | bytes 3932160 | tf_op jit(solution)/shard_map/halves/pallas_call | solution.py:91
  108.2 7.7 %all-to-all-start.5 = ((bf16[64,8,1920]{2,1,0:T(8,128)(2,1)}), bf16[64,8,1920]{2,1,0:T(8,128)(2,1)S(1)}, u32[]{:S(2)}, u32[]{:S(2)}) async-start(bf16[64,8,1920]{2,1,0:T(8,128)(2,1)} %halves.11), calls=%async_computation.11 | async-start | bytes 3932160 | tf_op jit(solution)/shard_map/all_to_all | solution.py:171
  116.8 17.3 %waves.7 = bf16[2,32,64,480]{3,2,1,0:T(8,128)(2,1)} custom-call(bf16[256,1024]{1,0:T(8,128)(2,1)} %pad_maximum_fusion.1.c_ref, bf16[32,480,1024]{2,1,0:T(8,128)(2,1)} %bitcast.65), custom_call_target="tpu_custom_call" | custom-call | flops 8053063680 | bytes 31457280 | tf_op jit(solution)/shard_map/waves/pallas_call | solution.py:61
  134.1 5.0 %halves.10 = bf16[64,8,1920]{2,1,0:T(8,128)(2,1)} custom-call(bf16[32,64,480]{2,1,0:T(8,128)(2,1)} %bitcast.72, bf16[480,480]{1,0:T(8,128)(2,1)} %maximum_maximum_fusion.t_ref), custom_call_target="tpu_custom_call" | custom-call | flops 943718400 | bytes 3932160 | tf_op jit(solution)/shard_map/halves/pallas_call | solution.py:91
  139.1 22.0 %all-to-all-done.5 = bf16[64,8,1920]{2,1,0:T(8,128)(2,1)S(1)} async-done(((bf16[64,8,1920]{2,1,0:T(8,128)(2,1)}), bf16[64,8,1920]{2,1,0:T(8,128)(2,1)S(1)}, u32[]{:S(2)}, u32[]{:S(2)}) %all-to-all-start.5) | async-done | bytes 1966112 | tf_op jit(solution)/shard_map/all_to_all | solution.py:171
  170.4 40.0 %all-to-all-done.4 = bf16[64,8,1920]{2,1,0:T(8,128)(2,1)} async-done(((bf16[64,8,1920]{2,1,0:T(8,128)(2,1)}), bf16[64,8,1920]{2,1,0:T(8,128)(2,1)}, u32[]{:S(2)}, u32[]{:S(2)}) %all-to-all-start.4) | async-done | bytes 1966112 | tf_op jit(solution)/shard_map/all_to_all | solution.py:171
  215.2 17.2 %waves.6 = bf16[2,32,64,480]{3,2,1,0:T(8,128)(2,1)} custom-call(bf16[256,1024]{1,0:T(8,128)(2,1)} %pad_maximum_fusion.c_ref, bf16[32,480,1024]{2,1,0:T(8,128)(2,1)} %bitcast.66), custom_call_target="tpu_custom_call" | custom-call | flops 8053063680 | bytes 31457280 | tf_op jit(solution)/shard_map/waves/pallas_call | solution.py:61
  232.5 5.0 %halves.8 = bf16[64,8,1920]{2,1,0:T(8,128)(2,1)} custom-call(bf16[32,64,480]{2,1,0:T(8,128)(2,1)} %bitcast.70, bf16[480,480]{1,0:T(8,128)(2,1)} %maximum_maximum_fusion.t_ref), custom_call_target="tpu_custom_call" | custom-call | flops 943718400 | bytes 3932160 | tf_op jit(solution)/shard_map/halves/pallas_call | solution.py:91
  237.5 22.2 %all-to-all-done.3 = bf16[64,8,1920]{2,1,0:T(8,128)(2,1)S(1)} async-done(((bf16[64,8,1920]{2,1,0:T(8,128)(2,1)}), bf16[64,8,1920]{2,1,0:T(8,128)(2,1)S(1)}, u32[]{:S(2)}, u32[]{:S(2)}) %all-to-all-start.3) | async-done | bytes 1966112 | tf_op jit(solution)/shard_map/all_to_all | solution.py:171
  269.0 40.1 %all-to-all-done.2 = bf16[64,8,1920]{2,1,0:T(8,128)(2,1)} async-done(((bf16[64,8,1920]{2,1,0:T(8,128)(2,1)}), bf16[64,8,1920]{2,1,0:T(8,128)(2,1)}, u32[]{:S(2)}, u32[]{:S(2)}) %all-to-all-start.2) | async-done | bytes 1966112 | tf_op jit(solution)/shard_map/all_to_all | solution.py:171
  312.7 5.0 %halves.6 = bf16[64,8,1920]{2,1,0:T(8,128)(2,1)} custom-call(bf16[32,64,480]{2,1,0:T(8,128)(2,1)} %bitcast.75, bf16[480,480]{1,0:T(8,128)(2,1)} %maximum_maximum_fusion.t_ref), custom_call_target="tpu_custom_call" | custom-call | flops 943718400 | bytes 3932160 | tf_op jit(solution)/shard_map/halves/pallas_call | solution.py:91
  317.7 40.6 %all-to-all-done.1 = bf16[64,8,1920]{2,1,0:T(8,128)(2,1)S(1)} async-done(((bf16[64,8,1920]{2,1,0:T(8,128)(2,1)}), bf16[64,8,1920]{2,1,0:T(8,128)(2,1)S(1)}, u32[]{:S(2)}, u32[]{:S(2)}) %all-to-all-start.1) | async-done | bytes 1966112 | tf_op jit(solution)/shard_map/all_to_all | solution.py:171
  364.6 7.4 %spectra.6.rest_0_ = f32[48,240,256]{2,1,0:T(8,128)} custom-call(bf16[8,8,8,1920]{3,2,1,0:T(8,128)(2,1)} %bitcast.67, bf16[256,512]{1,0:T(8,128)(2,1)} %fusion.48.t_ref), custom_call_target="tpu_custom_call" | custom-call | flops 1006632960 | bytes 3932160 | tf_op jit(solution)/shard_map/spectra/pallas_call | solution.py:130
  372.0 7.4 %spectra.7.rest_0_ = f32[48,240,256]{2,1,0:T(8,128)} custom-call(bf16[8,8,8,1920]{3,2,1,0:T(8,128)(2,1)} %bitcast.28.h_ref, bf16[256,512]{1,0:T(8,128)(2,1)} %fusion.48.t_ref, f32[48,240,256]{2,1,0:T(8,128)} %spectra.6.rest_0_), custom_call_target="tpu_custom_call", output_to_operand_aliasing={{}: (2, {})} | custom-call | flops 1006632960 | bytes 3932160 | tf_op jit(solution)/shard_map/spectra/pallas_call | solution.py:130
  379.3 7.4 %spectra.8.rest_0_ = f32[48,240,256]{2,1,0:T(8,128)} custom-call(bf16[8,8,8,1920]{3,2,1,0:T(8,128)(2,1)} %bitcast.68, bf16[256,512]{1,0:T(8,128)(2,1)} %fusion.48.t_ref, f32[48,240,256]{2,1,0:T(8,128)} %spectra.7.rest_0_), custom_call_target="tpu_custom_call", output_to_operand_aliasing={{}: (2, {})} | custom-call | flops 1006632960 | bytes 3932160 | tf_op jit(solution)/shard_map/spectra/pallas_call | solution.py:130
  386.7 7.4 %spectra.9.rest_0_ = f32[48,240,256]{2,1,0:T(8,128)} custom-call(bf16[8,8,8,1920]{3,2,1,0:T(8,128)(2,1)} %bitcast.18.h_ref, bf16[256,512]{1,0:T(8,128)(2,1)} %fusion.48.t_ref, f32[48,240,256]{2,1,0:T(8,128)} %spectra.8.rest_0_), custom_call_target="tpu_custom_call", output_to_operand_aliasing={{}: (2, {})} | custom-call | flops 1006632960 | bytes 3932160 | tf_op jit(solution)/shard_map/spectra/pallas_call | solution.py:130
  394.0 7.4 %spectra.10.rest_0_ = f32[48,240,256]{2,1,0:T(8,128)} custom-call(bf16[8,8,8,1920]{3,2,1,0:T(8,128)(2,1)} %bitcast.69, bf16[256,512]{1,0:T(8,128)(2,1)} %fusion.48.t_ref, f32[48,240,256]{2,1,0:T(8,128)} %spectra.9.rest_0_), custom_call_target="tpu_custom_call", output_to_operand_aliasing={{}: (2, {})} | custom-call | flops 1006632960 | bytes 3932160 | tf_op jit(solution)/shard_map/spectra/pallas_call | solution.py:130
  401.4 6.3 %all-to-all-done = bf16[64,8,1920]{2,1,0:T(8,128)(2,1)} async-done(((bf16[64,8,1920]{2,1,0:T(8,128)(2,1)}), bf16[64,8,1920]{2,1,0:T(8,128)(2,1)}, u32[]{:S(2)}, u32[]{:S(2)}) %all-to-all-start) | async-done | bytes 1966112 | tf_op jit(solution)/shard_map/all_to_all | solution.py:171
  407.7 7.4 %spectra.11 = f32[48,240,256]{2,1,0:T(8,128)} custom-call(bf16[8,8,8,1920]{3,2,1,0:T(8,128)(2,1)} %bitcast.8.h_ref, bf16[256,512]{1,0:T(8,128)(2,1)} %fusion.48.t_ref, f32[48,240,256]{2,1,0:T(8,128)} %spectra.10.rest_0_), custom_call_target="tpu_custom_call", output_to_operand_aliasing={{}: (2, {})} | custom-call | flops 1006632960 | bytes 3932160 | tf_op jit(solution)/shard_map/spectra/pallas_call | solution.py:130
  (53 shorter events, 43.5 us)
Async XLA Ops:
  6.5 96.7 %reduce-scatter.17.cloned.1.call-start = ((), (), s32[]{:S(2)}) async-start(), calls=%async_computation.17 | async-start | bytes 6291456 | tf_op jit(solution)/shard_map/reduce_scatter | solution.py:169
  42.9 91.2 %reduce-scatter.15.cloned.1.call-start = ((), (), s32[]{:S(2)}) async-start(), calls=%async_computation.16 | async-start | bytes 6291456 | tf_op jit(solution)/shard_map/reduce_scatter | solution.py:169
  61.9 103.6 %reduce-scatter.13.cloned.1.call-start = ((), (), s32[]{:S(2)}) async-start(), calls=%async_computation.15 | async-start | bytes 6291456 | tf_op jit(solution)/shard_map/reduce_scatter | solution.py:169
  81.0 151.5 %reduce-scatter.11.cloned.1.call-start = ((), (), s32[]{:S(2)}) async-start(), calls=%async_computation.14 | async-start | bytes 6291456 | tf_op jit(solution)/shard_map/reduce_scatter | solution.py:169
  108.2 52.9 %all-to-all-start.5 = ((bf16[64,8,1920]{2,1,0:T(8,128)(2,1)}), bf16[64,8,1920]{2,1,0:T(8,128)(2,1)S(1)}, u32[]{:S(2)}, u32[]{:S(2)}) async-start(bf16[64,8,1920]{2,1,0:T(8,128)(2,1)} %halves.11), calls=%async_computation.11 | async-start | bytes 3932160 | tf_op jit(solution)/shard_map/all_to_all | solution.py:171
  115.9 148.2 %reduce-scatter.9.cloned.1.call-start = ((), (), s32[]{:S(2)}) async-start(), calls=%async_computation.13 | async-start | bytes 6291456 | tf_op jit(solution)/shard_map/reduce_scatter | solution.py:169
  161.1 9.3 %copy-start = (bf16[64,8,1920]{2,1,0:T(8,128)(2,1)}, bf16[64,8,1920]{2,1,0:T(8,128)(2,1)S(1)}, u32[]{:S(2)}) copy-start(bf16[64,8,1920]{2,1,0:T(8,128)(2,1)S(1)} %all-to-all-done.5) | copy-start | bytes 5898244
  161.1 49.4 %all-to-all-start.4 = ((bf16[64,8,1920]{2,1,0:T(8,128)(2,1)}), bf16[64,8,1920]{2,1,0:T(8,128)(2,1)}, u32[]{:S(2)}, u32[]{:S(2)}) async-start(bf16[64,8,1920]{2,1,0:T(8,128)(2,1)} %halves.10), calls=%async_computation.9 | async-start | bytes 3932160 | tf_op jit(solution)/shard_map/all_to_all | solution.py:171
  210.5 49.2 %all-to-all-start.3 = ((bf16[64,8,1920]{2,1,0:T(8,128)(2,1)}), bf16[64,8,1920]{2,1,0:T(8,128)(2,1)S(1)}, u32[]{:S(2)}, u32[]{:S(2)}) async-start(bf16[64,8,1920]{2,1,0:T(8,128)(2,1)} %halves.9), calls=%async_computation.7 | async-start | bytes 3932160 | tf_op jit(solution)/shard_map/all_to_all | solution.py:171
  214.1 98.6 %reduce-scatter.7.cloned.1.call-start = ((), (), s32[]{:S(2)}) async-start(), calls=%async_computation.12 | async-start | bytes 6291456 | tf_op jit(solution)/shard_map/reduce_scatter | solution.py:169
  259.7 9.3 %copy-start.1 = (bf16[64,8,1920]{2,1,0:T(8,128)(2,1)}, bf16[64,8,1920]{2,1,0:T(8,128)(2,1)S(1)}, u32[]{:S(2)}) copy-start(bf16[64,8,1920]{2,1,0:T(8,128)(2,1)S(1)} %all-to-all-done.3) | copy-start | bytes 5898244
  259.7 49.4 %all-to-all-start.2 = ((bf16[64,8,1920]{2,1,0:T(8,128)(2,1)}), bf16[64,8,1920]{2,1,0:T(8,128)(2,1)}, u32[]{:S(2)}, u32[]{:S(2)}) async-start(bf16[64,8,1920]{2,1,0:T(8,128)(2,1)} %halves.8), calls=%async_computation.5 | async-start | bytes 3932160 | tf_op jit(solution)/shard_map/all_to_all | solution.py:171
  309.1 49.2 %all-to-all-start.1 = ((bf16[64,8,1920]{2,1,0:T(8,128)(2,1)}), bf16[64,8,1920]{2,1,0:T(8,128)(2,1)S(1)}, u32[]{:S(2)}, u32[]{:S(2)}) async-start(bf16[64,8,1920]{2,1,0:T(8,128)(2,1)} %halves.7), calls=%async_computation.3 | async-start | bytes 3932160 | tf_op jit(solution)/shard_map/all_to_all | solution.py:171
  358.3 5.6 %copy-start.2 = (bf16[64,8,1920]{2,1,0:T(8,128)(2,1)}, bf16[64,8,1920]{2,1,0:T(8,128)(2,1)S(1)}, u32[]{:S(2)}) copy-start(bf16[64,8,1920]{2,1,0:T(8,128)(2,1)S(1)} %all-to-all-done.1) | copy-start | bytes 5898244
  358.3 49.4 %all-to-all-start = ((bf16[64,8,1920]{2,1,0:T(8,128)(2,1)}), bf16[64,8,1920]{2,1,0:T(8,128)(2,1)}, u32[]{:S(2)}, u32[]{:S(2)}) async-start(bf16[64,8,1920]{2,1,0:T(8,128)(2,1)} %halves.6), calls=%async_computation.1 | async-start | bytes 3932160 | tf_op jit(solution)/shard_map/all_to_all | solution.py:171
Sparse Core Ops, SparseCore 0:
  43.0 14.7 reduce-scatter.16
  62.0 14.9 reduce-scatter.14
  81.1 14.9 reduce-scatter.12
  100.3 15.1 reduce-scatter.10
  134.2 13.4 reduce-scatter.8
  232.6 13.2 reduce-scatter.6
